TPU v7x, 512 devices: a whole 4x4x16 slice. The times are simulated.
512 devices in a mesh: tm: 16 (over z), chan: 16 (over y_lo, x, core), freq: 2 (over y_hi).
Axes of the slice: x: 4, y: 4 (y_hi: 2, y_lo: 2; y = y_hi * 2 + y_lo), z: 16, core: 2. Of those that a mesh axis runs over, the one named last changes fastest.
Arguments:
- raw_record: bfloat16 [32, 4096, 4096], P(('tm', 'freq'), 'chan'), may hold values from -6 to 6
- good_mask: int32 [4096], P('chan'), may hold values 0 or 1
- reach_limit: int32 [4096], P('chan'), may hold values from 128 to 511
Outputs:
- stacked_cross: bfloat16 [2, 128, 4096, 512], P(None, ('tm', 'freq'), 'chan')
All inputs are finite; a program needn't handle non-finite values. No bound on the sum of `good_mask` on one device may be relied on, other than what follows from the above.
Results may differ from a plain program's by a relative error of at most 0.0066.
Values may be sent and summed in bfloat16 or wider, within the bound.
A program may use at most 64 MiB of HBM per device.

v0:
```python
import jax
import jax.numpy as jnp
from jax import lax
from jax.sharding import PartitionSpec as P

K = 512
F0 = 64
FB_DEV = 4


def shifted(value, axis, by):
    peers = lax.axis_size(axis)
    pairs = [(i, i + by) for i in range(peers) if 0 <= i + by < peers]
    return lax.ppermute(value, axis, pairs)


def build_rows(groups, group_bins, length):
    count = groups * group_bins
    bins = F0 + jnp.arange(count, dtype=jnp.int32)
    times = jnp.arange(length, dtype=jnp.int32)
    phase = 2.0 * jnp.pi * (bins[:, None] * times[None, :] % length).astype(jnp.float32) / length
    taper = 0.5 - 0.5 * jnp.cos(2.0 * jnp.pi * times.astype(jnp.float32) / length)
    real_part = (taper[None, :] * jnp.cos(phase)).reshape(groups, group_bins, length)
    imag_part = (-taper[None, :] * jnp.sin(phase)).reshape(groups, group_bins, length)
    rows = jnp.stack([real_part, imag_part], axis=1).reshape(2 * count, length)
    return rows.astype(jnp.bfloat16)


def body(raw_record, good_mask, reach_limit):
    tm_count = lax.axis_size("tm")
    freq_count = lax.axis_size("freq")
    groups = tm_count * freq_count
    local_windows, block_width, length = raw_record.shape
    band_bins = groups * FB_DEV
    table = build_rows(groups, FB_DEV, length)
    samples = raw_record.reshape(local_windows * block_width, length)
    spectrum = lax.dot_general(
        table, samples, (((1,), (1,)), ((), ())), preferred_element_type=jnp.float32
    )
    spectrum = spectrum.reshape(groups, 2, FB_DEV, local_windows, block_width)
    power = jnp.sum(spectrum * spectrum, axis=(0, 1, 2)) / band_bins
    factor = lax.rsqrt(power + 1e-06) * good_mask.astype(jnp.float32)[None, :]
    white = (spectrum * factor[None, None, None]).astype(jnp.bfloat16)
    moved = lax.all_to_all(white, ("tm", "freq"), split_axis=0, concat_axis=3, tiled=True)
    own_block = moved.reshape(2, FB_DEV, groups * local_windows, block_width)
    block_count = -(-K // block_width)
    blocks = [own_block]
    for step in range(1, block_count + 1):
        blocks.append(shifted(own_block, "chan", -step))
    extended = jnp.concatenate(blocks, axis=3)
    width = extended.shape[3]
    left_side = jnp.concatenate([own_block[0], own_block[1]], axis=1)
    right_real = jnp.concatenate([extended[0], extended[1]], axis=1)
    right_imag = jnp.concatenate([extended[1], -extended[0]], axis=1)
    right_side = jnp.stack([right_real, right_imag])
    gram = jnp.einsum("fwc,pfwm->pfcm", left_side, right_side, preferred_element_type=jnp.float32)
    flat = jnp.pad(gram.reshape(2, FB_DEV, block_width * width), ((0, 0), (0, 0), (0, block_width)))
    band = flat.reshape(2, FB_DEV, block_width, width + 1)[:, :, :, :K]
    offsets = jnp.arange(K, dtype=jnp.int32)
    keep = offsets[None, :] <= reach_limit[:, None]
    return jnp.where(keep[None, None], band, 0.0).astype(jnp.bfloat16)


def solution(mesh):
    placed = (P(("tm", "freq"), "chan", None), P("chan"), P("chan"))
    return jax.shard_map(
        body,
        mesh=mesh,
        in_specs=placed,
        out_specs=P(None, ("tm", "freq"), "chan", None),
        check_vma=False,
    )
```

profile of v0, /device:TPU:1, one launch (start us, length us, event | category | flops | bytes accessed | tf_op | source)
XLA Modules:
  0.0 96.1 jit_solution(3340238058119404880)
XLA Ops:
  0.0 0.0 copy-start
  0.0 0.1 multiply_subtract_fusion
  0.1 8.7 %multiply_convert_fusion.1 = (bf16[32,1,4,4096]{3,0,2,1:T(8,128)(2,1)S(1)}, bf16[32,1,4,4096]{3,0,2,1:T(8,128)(2,1)S(1)}) fusion(s32[32,4]{0,1:T(4,128)S(1)} %add_add_fusion, f32[4096]{0:T(1024)S(1)} %get-tuple-element.17, f32[4096]{0:T(1024)S(1)} %get-tuple-element.18), kind=kLoop, calls=%fused_computation.13 | loop fusion | flops 9437184 | bytes 2130432 | tf_op jit(solution)/shard_map/convert
  8.8 0.2 pad_maximum_fusion
  9.0 2.9 %copy.17 = bf16[32,2,4,4096]{3,2,1,0:T(4,128)(2,1)} copy(bf16[32,2,4,4096]{3,0,2,1:T(8,128)(2,1)S(1)} %pad_maximum_fusion) | data formatting | bytes 4194304 | tf_op jit(solution)/shard_map/stack | solution.py:25
  11.9 4.0 %convert_element_type.59 = bf16[256,4096]{1,0:T(8,128)(2,1)} reshape(bf16[32,2,4,4096]{3,2,1,0:T(4,128)(2,1)} %copy.17) | data formatting | bytes 4194304 | tf_op jit(solution)/shard_map/convert_element_type | solution.py:26
  15.9 0.0 copy-done
  15.9 0.0 copy-start.2
  15.9 0.0 copy-start.1
  15.9 2.4 %multiply_reduce_fusion = (f32[256]{0:T(256)S(1)}, f32[256,256]{1,0:T(8,128)S(1)}) fusion(bf16[256,4096]{1,0:T(8,128)(2,1)} %convert_element_type.59, bf16[1,256,4096]{2,1,0:T(8,128)(2,1)S(1)} %copy-done), kind=kOutput, calls=%fused_computation.25 | convolution fusion | flops 537001728 | bytes 4457472 | tf_op jit(solution)/shard_map/dot_general | solution.py:37
  18.3 0.1 reshape.180
  18.4 0.0 copy-done.2
  18.4 0.1 fusion.10
  18.5 0.8 copy.19
  19.2 18.7 %all-to-all-start = ((bf16[32,2,4,1,256]{4,2,1,3,0:T(4,128)(2,1)}), bf16[32,2,4,1,256]{4,2,1,3,0:T(4,128)(2,1)S(1)}, u32[]{:S(2)}, u32[]{:S(2)}) async-start(bf16[32,2,4,1,256]{4,2,1,3,0:T(4,128)(2,1)} %copy.19), calls=%async_computation | async-start | bytes 262144 | tf_op jit(solution)/shard_map/all_to_all | solution.py:44
  37.9 0.0 copy-done.1
  37.9 0.1 iota_compare_fusion
  38.0 14.6 %all-to-all-done = bf16[32,2,4,1,256]{4,2,1,3,0:T(4,128)(2,1)S(1)} async-done(((bf16[32,2,4,1,256]{4,2,1,3,0:T(4,128)(2,1)}), bf16[32,2,4,1,256]{4,2,1,3,0:T(4,128)(2,1)S(1)}, u32[]{:S(2)}, u32[]{:S(2)}) %all-to-all-start) | async-done | bytes 131104 | tf_op jit(solution)/shard_map/all_to_all | solution.py:44
  52.7 5.6 %collective-permute-start = (bf16[2,4,32,256]{3,2,1,0:T(8,128)(2,1)S(1)}, bf16[2,4,32,256]{3,2,1,0:T(8,128)(2,1)S(1)}, u32[]{:S(2)}, u32[]{:S(2)}) collective-permute-start(bf16[2,4,32,256]{3,2,1,0:T(8,128)(2,1)S(1)} %bitcast.37), channel_id=1, source_target_pairs={{2,0},{4,2},{6,4},{8,6},{10,8},{12,10},{14,12},{16,14},{18,16},{20... | collective-permute-start | bytes 393224 | tf_op jit(solution)/shard_map/ppermute | solution.py:14
  58.3 1.5 %collective-permute-start.1 = (bf16[2,4,32,256]{3,2,1,0:T(8,128)(2,1)S(1)}, bf16[2,4,32,256]{3,2,1,0:T(8,128)(2,1)S(1)}, u32[]{:S(2)}, u32[]{:S(2)}) collective-permute-start(bf16[2,4,32,256]{3,2,1,0:T(8,128)(2,1)S(1)} %bitcast.38), channel_id=1, source_target_pairs={{4,0},{6,2},{8,4},{10,6},{12,8},{14,10},{16,12},{18,14},{20,16},{2... | collective-permute-start | bytes 393224 | tf_op jit(solution)/shard_map/ppermute | solution.py:14
  59.8 2.2 %collective-permute-done = bf16[2,4,32,256]{3,2,1,0:T(8,128)(2,1)S(1)} collective-permute-done((bf16[2,4,32,256]{3,2,1,0:T(8,128)(2,1)S(1)}, bf16[2,4,32,256]{3,2,1,0:T(8,128)(2,1)S(1)}, u32[]{:S(2)}, u32[]{:S(2)}) %collective-permute-start) | collective-permute-done | bytes 131104 | tf_op jit(solution)/shard_map/ppermute | solution.py:14
  62.1 3.6 %collective-permute-done.1 = bf16[2,4,32,256]{3,2,1,0:T(8,128)(2,1)S(1)} collective-permute-done((bf16[2,4,32,256]{3,2,1,0:T(8,128)(2,1)S(1)}, bf16[2,4,32,256]{3,2,1,0:T(8,128)(2,1)S(1)}, u32[]{:S(2)}, u32[]{:S(2)}) %collective-permute-start.1) | collective-permute-done | bytes 131104 | tf_op jit(solution)/shard_map/ppermute | solution.py:14
  65.7 0.1 maximum_bitcast_fusion
  65.8 2.7 %convolution_bitcast_fusion = bf16[2,4,256,768]{2,3,0,1:T(8,128)(2,1)} fusion(bf16[4,32,256]{2,1,0:T(8,128)(2,1)S(1)} %get-tuple-element.10, bf16[4,32,256]{2,1,0:T(8,128)(2,1)S(1)} %get-tuple-element.9, bf16[1,4,64,768]{3,2,1,0:T(8,128)(2,1)S(1)} %get-tuple-element.8, bf16[1,4,64,768]{3,2,1,0:T(8,128)(2,1)S(1)} %get-tuple-element.7), kind=kOutput, calls=%fused_computation.5 | convolution fusion | flops 201981952 | bytes 4063232 | tf_op jit(solution)/shard_map/fwc,pfwm->pfcm/dot_general | solution.py:56
  68.5 4.6 %copy.22 = bf16[2,4,256,768]{3,2,1,0:T(8,128)(2,1)} copy(bf16[2,4,256,768]{2,3,0,1:T(8,128)(2,1)} %convolution_bitcast_fusion) | data formatting | bytes 6291456 | tf_op jit(solution)/shard_map/fwc,pfwm->pfcm/transpose | solution.py:56
  73.2 5.0 %reshape.182 = bf16[2,4,196608]{2,1,0:T(4,128)(2,1)} reshape(bf16[2,4,256,768]{3,2,1,0:T(8,128)(2,1)} %copy.22) | data formatting | bytes 6291456 | tf_op jit(solution)/shard_map/reshape | solution.py:57
  78.1 5.0 %pad.4 = bf16[2,4,196864]{2,1,0:T(4,128)(2,1)} pad(bf16[2,4,196608]{2,1,0:T(4,128)(2,1)} %reshape.182, bf16[]{:T(256)} %constant.77), padding=0_0x0_0x0_256 | pad | bytes 6295554 | tf_op jit(solution)/shard_map/jit(_pad)/pad | solution.py:57
  83.2 9.5 %reshape.183 = bf16[2,4,256,769]{3,2,1,0:T(8,128)(2,1)} reshape(bf16[2,4,196864]{2,1,0:T(4,128)(2,1)} %pad.4) | data formatting | bytes 6299648 | tf_op jit(solution)/shard_map/reshape | solution.py:58
  92.7 3.4 %fusion = bf16[2,4,256,512]{3,2,1,0:T(8,128)(2,1)} fusion(bf16[2,4,256,769]{3,2,1,0:T(8,128)(2,1)} %reshape.183, pred[256,512]{1,0:T(8,128)(4,1)S(1)} %iota_compare_fusion), kind=kLoop, calls=%fused_computation.1 | loop fusion | flops 1048576 | bytes 4325376 | tf_op jit(solution)/shard_map/convert_element_type | solution.py:61
  (7 shorter events, 0.1 us)
Async XLA Ops:
  0.0 15.9 %copy-start = (bf16[1,256,4096]{2,1,0:T(8,128)(2,1)S(1)}, bf16[1,256,4096]{2,1,0:T(8,128)(2,1)}, u32[]{:S(2)}) copy-start(bf16[1,256,4096]{2,1,0:T(8,128)(2,1)} %param.3) | copy-start | bytes 6291460
  15.9 2.5 %copy-start.2 = (s32[256]{0:T(256)S(1)}, s32[256]{0:T(256)}, u32[]{:S(2)}) copy-start(s32[256]{0:T(256)} %param.4) | copy-start | bytes 3076
  15.9 22.0 %copy-start.1 = (s32[256]{0:T(256)S(1)}, s32[256]{0:T(256)}, u32[]{:S(2)}) copy-start(s32[256]{0:T(256)} %param.5) | copy-start | bytes 3076
  19.2 33.4 %all-to-all-start = ((bf16[32,2,4,1,256]{4,2,1,3,0:T(4,128)(2,1)}), bf16[32,2,4,1,256]{4,2,1,3,0:T(4,128)(2,1)S(1)}, u32[]{:S(2)}, u32[]{:S(2)}) async-start(bf16[32,2,4,1,256]{4,2,1,3,0:T(4,128)(2,1)} %copy.19), calls=%async_computation | async-start | bytes 262144 | tf_op jit(solution)/shard_map/all_to_all | solution.py:44
  52.7 9.4 %collective-permute-start = (bf16[2,4,32,256]{3,2,1,0:T(8,128)(2,1)S(1)}, bf16[2,4,32,256]{3,2,1,0:T(8,128)(2,1)S(1)}, u32[]{:S(2)}, u32[]{:S(2)}) collective-permute-start(bf16[2,4,32,256]{3,2,1,0:T(8,128)(2,1)S(1)} %bitcast.37), channel_id=1, source_target_pairs={{2,0},{4,2},{6,4},{8,6},{10,8},{12,10},{14,12},{16,14},{18,16},{20... | collective-permute-start | bytes 393224 | tf_op jit(solution)/shard_map/ppermute | solution.py:14
  58.3 7.3 %collective-permute-start.1 = (bf16[2,4,32,256]{3,2,1,0:T(8,128)(2,1)S(1)}, bf16[2,4,32,256]{3,2,1,0:T(8,128)(2,1)S(1)}, u32[]{:S(2)}, u32[]{:S(2)}) collective-permute-start(bf16[2,4,32,256]{3,2,1,0:T(8,128)(2,1)S(1)} %bitcast.38), channel_id=1, source_target_pairs={{4,0},{6,2},{8,4},{10,6},{12,8},{14,10},{16,12},{18,14},{20,16},{2... | collective-permute-start | bytes 393224 | tf_op jit(solution)/shard_map/ppermute | solution.py:14
where the time goes:
time: 97.7 us; the launch traced here: 96.1 us
  local copies, waits for them, and re-layouts  32 us (33%)
  starting transfers between devices  25.8 us (26%)
  waiting for transfers between devices  20.4 us (21%)
  other arithmetic  12.7 us (13%)
  matrix products  5.1 us (5%)
    all_to_all x1, starting transfers between devices, body(): lax.all_to_all(white, ('tm', 'freq'), split_axis=0, concat_axis=3, tiled=...  18.7 us
    all_to_all x1, waiting for transfers between devices, body(): lax.all_to_all(white, ('tm', 'freq'), split_axis=0, concat_axis=3, tiled=...  14.6 us
    reshape x1, local copies, waits for them, and re-layouts, body(): band = flat.reshape(2, FB_DEV, block_width, width + 1)[:, :, :, :K]  9.53 us
    another operation x1, other arithmetic  8.68 us
    ppermute x2, starting transfers between devices, shifted(): return lax.ppermute(value, axis, pairs)  7.12 us
    ppermute x2, waiting for transfers between devices, shifted(): return lax.ppermute(value, axis, pairs)  5.81 us
    pad x1, local copies, waits for them, and re-layouts, body(): jnp.pad(gram.reshape(2, FB_DEV, block_width * width), ((0, 0), (0, 0), (0...  5.04 us
    reshape x1, local copies, waits for them, and re-layouts, body(): gram.reshape(2, FB_DEV, block_width * width)  5 us
  transfers between devices with their start and end apart: 3, of which 3 were waited for; matrix products, arithmetic and copies ran while one was open for 0% of the time, Pallas kernels for 0%

commit v1 on v0

v1 whole, which is shorter than its diff:
```python
import functools

import jax
import jax.numpy as jnp
import numpy as np
from jax import lax
from jax.experimental import pallas as pl
from jax.experimental.pallas import tpu as pltpu
from jax.sharding import PartitionSpec as P

K = 512
F0 = 64
FB_DEV = 4
ROWS = 2 * FB_DEV
LANES = 128
TIME_CHUNKS = 4
PARTS = 4
MESH = pl.DeviceIdType.MESH


def build_rows(groups, length):
    bins = F0 + np.arange(groups * FB_DEV, dtype=np.int64)
    times = np.arange(length, dtype=np.int64)
    turn = np.float32(2.0 * np.pi)
    phase = turn * ((bins[:, None] * times[None, :]) % length).astype(np.float32) / np.float32(length)
    taper = np.float32(0.5) - np.float32(0.5) * np.cos(turn * times.astype(np.float32) / np.float32(length))
    real_part = (taper[None, :] * np.cos(phase)).reshape(groups, FB_DEV, length)
    imag_part = (-taper[None, :] * np.sin(phase)).reshape(groups, FB_DEV, length)
    rows = np.stack([real_part, imag_part], axis=1).reshape(groups * ROWS, length)
    return rows.reshape(groups * ROWS, length // LANES, LANES).transpose(1, 0, 2).astype(jnp.bfloat16)


def ring_order(count):
    return sorted(range(1, count), key=lambda d: -min(d, count - d))


def exchange_kernel(tm_count, chan_count, freq_count, table_ref, raw_ref, mask_ref, out_ref,
                    table_v, raw_v, mask_v, send_v, recv_v, load_sem, mask_sem, send_sem, recv_sem, ahead_send, ahead_recv, out_sem):
    tm, chan, freq = lax.axis_index("tm"), lax.axis_index("chan"), lax.axis_index("freq")
    groups = tm_count * freq_count
    peers = [(dt, df) for dt in ring_order(tm_count) for df in range(freq_count)]
    peers += [(0, df) for df in range(1, freq_count)]

    def place(dt, df):
        return lax.rem(tm + dt, tm_count), lax.rem(freq + df, freq_count)

    barrier = pltpu.get_barrier_semaphore()
    for dt, df in peers:
        t, f = place(dt, df)
        pl.semaphore_signal(barrier, inc=1, device_id=(t, chan, f), device_id_type=MESH)
    for up in (1, 2):
        @pl.when(chan + up < chan_count)
        def _():
            pl.semaphore_signal(barrier, inc=1, device_id=(tm, chan + up, freq), device_id_type=MESH)

    length = raw_ref.shape[1]
    step = length // TIME_CHUNKS
    loads = []
    for i in range(TIME_CHUNKS):
        span = pl.ds(i * step, step)
        runs = pl.ds(i * step // LANES, step // LANES)
        loads.append((
            pltpu.make_async_copy(table_ref.at[runs], table_v.at[runs], load_sem.at[0, i]),
            pltpu.make_async_copy(raw_ref.at[:, span], raw_v.at[:, span], load_sem.at[1, i]),
        ))
    for pair in loads:
        for copy in pair:
            copy.start()
    mask_copy = pltpu.make_async_copy(mask_ref, mask_v, mask_sem)
    mask_copy.start()

    for up in (1, 2):
        @pl.when(chan + up >= chan_count)
        def _():
            recv_v[up] = jnp.zeros(recv_v.shape[1:], recv_v.dtype)

    spectrum = None
    for i, pair in enumerate(loads):
        for copy in pair:
            copy.wait()
        span = slice(i * step, (i + 1) * step)
        rows = jnp.concatenate([table_v[j] for j in range(i * step // LANES, (i + 1) * step // LANES)], axis=1)
        term = lax.dot_general(
            rows, raw_v[:, span], (((1,), (1,)), ((), ())), preferred_element_type=jnp.float32
        )
        spectrum = term if spectrum is None else spectrum + term
    power = jnp.sum(spectrum * spectrum, axis=0, keepdims=True) / (groups * FB_DEV)
    mask_copy.wait()
    factor = lax.rsqrt(power + 1e-06) * mask_v[...].astype(jnp.float32)
    white = (spectrum * factor).reshape(groups, ROWS, 2 * LANES)
    tiles = jnp.concatenate([white[:, :, :LANES], white[:, :, LANES:]], axis=1)
    send_v[...] = tiles.astype(jnp.bfloat16)

    def part_of(slot):
        return slot * PARTS // groups

    own = tm * freq_count + freq
    recv_v[0, 0] = send_v[own]

    pl.semaphore_wait(barrier, groups - 1 + jnp.minimum(chan, 2))
    sends = []
    for dt, df in peers:
        t, f = place(dt, df)
        slot = ((-dt) % tm_count) * freq_count + (-df) % freq_count
        copy = pltpu.make_async_remote_copy(
            src_ref=send_v.at[t * freq_count + f],
            dst_ref=recv_v.at[0, slot],
            send_sem=send_sem,
            recv_sem=recv_sem.at[part_of(slot)],
            device_id=(t, chan, f),
            device_id_type=MESH,
        )
        copy.start()
        sends.append(copy)

    per_part = groups // PARTS

    def ahead(up, q):
        span = pl.ds(q * per_part, per_part)
        return pltpu.make_async_remote_copy(
            src_ref=recv_v.at[0, span],
            dst_ref=recv_v.at[up, span],
            send_sem=ahead_send.at[up - 1, q],
            recv_sem=ahead_recv.at[up - 1, q],
            device_id=(tm, chan - up, freq),
            device_id_type=MESH,
        )

    def store(block, q):
        span = pl.ds(q * per_part, per_part)
        return pltpu.make_async_copy(recv_v.at[block, span], out_ref.at[block, span], out_sem.at[block, q])

    for q in range(PARTS):
        lo = 1 if q == 0 else q * per_part
        span = pl.ds(lo, (q + 1) * per_part - lo)
        pltpu.make_async_copy(recv_v.at[0, span], recv_v.at[0, span], recv_sem.at[q]).wait()
        for up in (1, 2):
            @pl.when(chan >= up)
            def _():
                ahead(up, q).start()
        store(0, q).start()
    for q in range(PARTS):
        for up in (1, 2):
            @pl.when(chan + up < chan_count)
            def _():
                ahead(up, q).wait_recv()
            store(up, q).start()
    rest = pl.ds(1, groups - 1)
    pltpu.make_async_copy(send_v.at[rest], send_v.at[rest], send_sem).wait()
    for q in range(PARTS):
        for up in (1, 2):
            @pl.when(chan >= up)
            def _():
                ahead(up, q).wait_send()
        for block in range(3):
            store(block, q).wait()


def exchange(table, raw, mask, tm_count, chan_count, freq_count):
    groups = tm_count * freq_count
    width, length = raw.shape
    return pl.pallas_call(
        functools.partial(exchange_kernel, tm_count, chan_count, freq_count),
        out_shape=jax.ShapeDtypeStruct((3, groups, 2 * ROWS, LANES), jnp.bfloat16),
        in_specs=[
            pl.BlockSpec(memory_space=pltpu.HBM),
            pl.BlockSpec(memory_space=pltpu.HBM),
            pl.BlockSpec(memory_space=pltpu.HBM),
        ],
        out_specs=pl.BlockSpec(memory_space=pl.ANY),
        scratch_shapes=[
            pltpu.VMEM(table.shape, jnp.bfloat16),
            pltpu.VMEM((width, length), jnp.bfloat16),
            pltpu.VMEM((1, width), jnp.int32),
            pltpu.VMEM((groups, 2 * ROWS, LANES), jnp.bfloat16),
            pltpu.VMEM((3, groups, 2 * ROWS, LANES), jnp.bfloat16),
            pltpu.SemaphoreType.DMA((2, TIME_CHUNKS)),
            pltpu.SemaphoreType.DMA,
            pltpu.SemaphoreType.DMA,
            pltpu.SemaphoreType.DMA((PARTS,)),
            pltpu.SemaphoreType.DMA((2, PARTS)),
            pltpu.SemaphoreType.DMA((2, PARTS)),
            pltpu.SemaphoreType.DMA((3, PARTS)),
        ],
        compiler_params=pltpu.CompilerParams(
            collective_id=0, has_side_effects=True, vmem_limit_bytes=60 << 20
        ),
        name="exchange",
    )(table, raw, mask)


def band_kernel(blocks_ref, reach_ref, out_ref, right_v, left_v, reach_v):
    depth = right_v.shape[0]
    groups = depth // ROWS
    index = pl.program_id(0)

    @pl.when(index == 0)
    def _():
        halves = []
        for block in range(3):
            tiles = blocks_ref[block].astype(jnp.float32)
            for half in range(2):
                halves.append(tiles[:, half * ROWS:(half + 1) * ROWS, :])
        for j, half in enumerate(halves):
            right_v[:, j * LANES:(j + 1) * LANES] = half.reshape(depth, LANES).astype(jnp.bfloat16)
        row = lax.broadcasted_iota(jnp.int32, (groups, ROWS, LANES), 1)
        for j in range(2):
            span = slice(j * LANES, (j + 1) * LANES)
            left_v[0, span, :] = halves[j].reshape(depth, LANES).T
            turned = jnp.concatenate([-halves[j][:, FB_DEV:], halves[j][:, :FB_DEV]], axis=1)
            left_v[1, span, :] = turned.reshape(depth, LANES).T
        reach_v[...] = jnp.broadcast_to(reach_ref[...], (LANES, 2 * LANES)).T

    part = index // FB_DEV
    which = lax.rem(index, FB_DEV)
    column = lax.broadcasted_iota(jnp.int32, (2 * LANES, depth), 1)
    left = jnp.where(lax.rem(column, FB_DEV) == which, left_v[part], 0.0).astype(jnp.bfloat16)
    row = lax.broadcasted_iota(jnp.int32, (LANES, LANES), 0)
    lane = lax.broadcasted_iota(jnp.int32, (LANES, LANES), 1)
    for half in range(2):
        rows = slice(half * LANES, (half + 1) * LANES)
        reach = reach_v[rows, :]
        count = K // LANES + 1
        turned = []
        for j in range(count):
            at = (half + j) * LANES
            product = jnp.dot(left[rows], right_v[:, at:at + LANES], preferred_element_type=jnp.float32)
            turned.append(jnp.take_along_axis(product, lax.rem(lane + row, LANES), axis=1, mode="promise_in_bounds"))
        for j in range(count - 1):
            band = jnp.where(lane + row < LANES, turned[j], turned[j + 1])
            band = jnp.where(lane + j * LANES <= reach, band, 0.0)
            out_ref[0, 0, rows, j * LANES:(j + 1) * LANES] = band.astype(out_ref.dtype)


def band_of(blocks, reach):
    groups = blocks.shape[1]
    depth = groups * ROWS
    return pl.pallas_call(
        band_kernel,
        grid=(2 * FB_DEV,),
        out_shape=jax.ShapeDtypeStruct((2, FB_DEV, 2 * LANES, K), jnp.bfloat16),
        in_specs=[
            pl.BlockSpec(blocks.shape, lambda i: (0, 0, 0, 0)),
            pl.BlockSpec((1, 2 * LANES), lambda i: (0, 0)),
        ],
        out_specs=pl.BlockSpec((1, 1, 2 * LANES, K), lambda i: (i // FB_DEV, i % FB_DEV, 0, 0)),
        scratch_shapes=[
            pltpu.VMEM((depth, 6 * LANES), jnp.bfloat16),
            pltpu.VMEM((2, 2 * LANES, depth), jnp.float32),
            pltpu.VMEM((2 * LANES, LANES), jnp.int32),
        ],
        name="band",
    )(blocks, reach)


def body(table, raw_record, good_mask, reach_limit):
    tm_count, chan_count, freq_count = (lax.axis_size(a) for a in ("tm", "chan", "freq"))
    width = raw_record.shape[1]
    blocks = exchange(table, raw_record[0], good_mask.reshape(1, width), tm_count, chan_count, freq_count)
    return band_of(blocks, reach_limit.reshape(1, width))


def solution(mesh):
    groups = mesh.shape["tm"] * mesh.shape["freq"]
    sharded = jax.shard_map(
        body,
        mesh=mesh,
        in_specs=(P(), P(("tm", "freq"), "chan", None), P("chan"), P("chan")),
        out_specs=P(None, ("tm", "freq"), "chan", None),
        check_vma=False,
    )

    def run(raw_record, good_mask, reach_limit):
        table = jnp.asarray(build_rows(groups, raw_record.shape[2]))
        return sharded(table, raw_record, good_mask, reach_limit)

    return run
```

time: 97.7 us -> 38.4 us (0.39); the launches traced: 96.1 us -> 38.3 us
  Pallas kernels: 0 us -> 38.3 us
  local copies, waits for them, and re-layouts: 32 us -> 0 us
  starting transfers between devices: 25.8 us -> 0 us
  waiting for transfers between devices: 20.4 us -> 0 us
  other arithmetic: 12.7 us -> 0 us
  matrix products: 5.1 us -> 0 us
    pallas_call x0 -> x2, Pallas kernels: none -> 38.3 us  [the longest x1 31.9 us: exchange(): pl.pallas_call(functools.partial(exchange_kernel, tm_count, chan_count, f...]
    all_to_all x1 -> x0, starting transfers between devices: 18.7 us -> none  [body(): lax.all_to_all(white, ('tm', 'freq'), split_axis=0, concat_axis=3, tiled=...]
    reshape x3 -> x0, local copies, waits for them, and re-layouts: 14.6 us -> none  [the longest x1 9.53 us: body(): band = flat.reshape(2, FB_DEV, block_width, width + 1)[:, :, :, :K]]
    all_to_all x1 -> x0, waiting for transfers between devices: 14.6 us -> none  [body(): lax.all_to_all(white, ('tm', 'freq'), split_axis=0, concat_axis=3, tiled=...]
    another operation x3 -> x0, other arithmetic: 8.94 us -> none
    ppermute x2 -> x0, starting transfers between devices: 7.12 us -> none  [shifted(): return lax.ppermute(value, axis, pairs)]
    ppermute x2 -> x0, waiting for transfers between devices: 5.81 us -> none  [shifted(): return lax.ppermute(value, axis, pairs)]
    dot_general x2 -> x0, matrix products: 5.1 us -> none  [the longest x1 2.72 us: body(): jnp.einsum('fwc,pfwm->pfcm', left_side, right_side, preferred_element_typ...]
  transfers between devices with their start and end apart: 3 -> 0, of which waited for: 3 -> 0; matrix products, arithmetic and copies ran while one was open for 0% -> 0% of each run, Pallas kernels for 0% -> 0%
where the time goes in v1:
time: 38.4 us; the launch traced here: 38.3 us
  Pallas kernels  38.3 us (100%)
    pallas_call x1, Pallas kernels, exchange(): pl.pallas_call(functools.partial(exchange_kernel, tm_count, chan_count, f...  31.9 us
    pallas_call x1, Pallas kernels, band_of(): pl.pallas_call(band_kernel, grid=(2 * FB_DEV,), out_shape=jax.ShapeDtypeS...  6.36 us

profile of v1, /device:TPU:1, one launch (start us, length us, event | category | flops | bytes accessed | tf_op | source)
XLA Modules:
  0.0 38.3 jit_solution(5217618727058842253)
XLA Ops:
  0.0 31.9 %exchange.1.blocks_ref = bf16[3,32,16,128]{3,2,1,0:T(8,128)(2,1)} custom-call(bf16[32,256,128]{2,1,0:T(8,128)(2,1)} %constant.2.clone.table_ref, bf16[256,4096]{1,0:T(8,128)(2,1)} %bitcast.3, s32[1,256]{1,0:T(1,128)} %bitcast.4), custom_call_target="tpu_custom_call" | custom-call | tf_op jit(solution)/shard_map/exchange/pallas_call | solution.py:162
  32.0 6.4 %band.1 = bf16[2,4,256,512]{3,2,1,0:T(8,128)(2,1)} custom-call(bf16[3,32,16,128]{3,2,1,0:T(8,128)(2,1)} %exchange.1.blocks_ref, s32[1,256]{1,0:T(1,128)} %bitcast.5), custom_call_target="tpu_custom_call" | custom-call | tf_op jit(solution)/shard_map/band/pallas_call | solution.py:238

commit v2 on v1

v2 whole, which is shorter than its diff:
```python
import functools

import jax
import jax.numpy as jnp
import numpy as np
from jax import lax
from jax.experimental import pallas as pl
from jax.experimental.pallas import tpu as pltpu
from jax.sharding import PartitionSpec as P

K = 512
F0 = 64
FB_DEV = 4
ROWS = 2 * FB_DEV
LANES = 128
TIME_CHUNKS = 4
PARTS = 4
MESH = pl.DeviceIdType.MESH


def build_rows(groups, length):
    bins = F0 + np.arange(groups * FB_DEV, dtype=np.int64)
    times = np.arange(length, dtype=np.int64)
    turn = np.float32(2.0 * np.pi)
    phase = turn * ((bins[:, None] * times[None, :]) % length).astype(np.float32) / np.float32(length)
    taper = np.float32(0.5) - np.float32(0.5) * np.cos(turn * times.astype(np.float32) / np.float32(length))
    real_part = (taper[None, :] * np.cos(phase)).reshape(groups, FB_DEV, length)
    imag_part = (-taper[None, :] * np.sin(phase)).reshape(groups, FB_DEV, length)
    rows = np.stack([real_part, imag_part], axis=1).reshape(groups * ROWS, length)
    return rows.reshape(groups * ROWS, length // LANES, LANES).transpose(1, 0, 2).astype(jnp.bfloat16)


def rank_of(distance, count):
    return jnp.maximum(jnp.minimum(2 * distance - 1, 2 * (count - distance)), 0)


def exchange_kernel(tm_count, chan_count, freq_count, table_ref, raw_ref, mask_ref, blocks_ref,
                    table_v, raw_v, mask_v, send_v, load_sem, mask_sem, send_sem, recv_sem, ahead_send, ahead_recv):
    tm, chan, freq = lax.axis_index("tm"), lax.axis_index("chan"), lax.axis_index("freq")
    groups = tm_count * freq_count
    per_part = groups // PARTS

    peers = [(tm, lax.rem(freq + df, freq_count), 0, df) for df in range(1, freq_count)]
    for k in range(tm_count - 1):
        t = k + jnp.minimum(jnp.maximum(k + 1 - tm, 0), 1)
        rank = rank_of(lax.rem(tm - t + tm_count, tm_count), tm_count)
        peers += [(t, lax.rem(freq + df, freq_count), rank, df) for df in range(freq_count)]

    length = raw_ref.shape[1]
    step = length // TIME_CHUNKS
    loads = []
    for i in range(TIME_CHUNKS):
        span = pl.ds(i * step, step)
        runs = pl.ds(i * step // LANES, step // LANES)
        loads.append((
            pltpu.make_async_copy(table_ref.at[runs], table_v.at[runs], load_sem.at[0, i]),
            pltpu.make_async_copy(raw_ref.at[:, span], raw_v.at[:, span], load_sem.at[1, i]),
        ))
    for pair in loads:
        for copy in pair:
            copy.start()
    mask_copy = pltpu.make_async_copy(mask_ref, mask_v, mask_sem)
    mask_copy.start()

    barrier = pltpu.get_barrier_semaphore()
    for t, f, _, _ in peers:
        pl.semaphore_signal(barrier, inc=1, device_id=(t, chan, f), device_id_type=MESH)
    for up in (1, 2):
        @pl.when(chan + up < chan_count)
        def _():
            pl.semaphore_signal(barrier, inc=1, device_id=(tm, chan + up, freq), device_id_type=MESH)

    for up in (1, 2):
        @pl.when(chan + up >= chan_count)
        def _():
            blocks_ref[up] = jnp.zeros(blocks_ref.shape[1:], blocks_ref.dtype)

    spectrum = None
    for i, pair in enumerate(loads):
        for copy in pair:
            copy.wait()
        rows = jnp.concatenate([table_v[j] for j in range(i * step // LANES, (i + 1) * step // LANES)], axis=1)
        term = lax.dot_general(
            rows, raw_v[:, i * step:(i + 1) * step], (((1,), (1,)), ((), ())), preferred_element_type=jnp.float32
        )
        spectrum = term if spectrum is None else spectrum + term
    power = jnp.sum(spectrum * spectrum, axis=0, keepdims=True) / (groups * FB_DEV)
    mask_copy.wait()
    factor = lax.rsqrt(power + 1e-06) * mask_v[...].astype(jnp.float32)
    white = (spectrum * factor).reshape(groups, ROWS, 2 * LANES)
    tiles = jnp.concatenate([white[:, :, :LANES], white[:, :, LANES:]], axis=1)
    send_v[...] = tiles.astype(jnp.bfloat16)

    pl.semaphore_wait(barrier, groups - 1 + jnp.minimum(chan, 2))
    for t, f, rank, df in peers:
        pltpu.make_async_remote_copy(
            src_ref=send_v.at[t * freq_count + f],
            dst_ref=blocks_ref.at[0, rank * freq_count + df],
            send_sem=send_sem,
            recv_sem=recv_sem.at[rank * freq_count // per_part],
            device_id=(t, chan, f),
            device_id_type=MESH,
        ).start()
    blocks_ref[0, 0] = send_v[tm * freq_count + freq]

    def ahead(up, q):
        span = pl.ds(q * per_part, per_part)
        return pltpu.make_async_remote_copy(
            src_ref=blocks_ref.at[0, span],
            dst_ref=blocks_ref.at[up, span],
            send_sem=ahead_send.at[up - 1, q],
            recv_sem=ahead_recv.at[up - 1, q],
            device_id=(tm, chan - up, freq),
            device_id_type=MESH,
        )

    for q in range(PARTS):
        lo = 1 if q == 0 else q * per_part
        span = pl.ds(lo, (q + 1) * per_part - lo)
        pltpu.make_async_copy(blocks_ref.at[0, span], blocks_ref.at[0, span], recv_sem.at[q]).wait()
        for up in (2, 1):
            @pl.when(chan >= up)
            def _():
                ahead(up, q).start()
    for q in range(PARTS):
        for up in (1, 2):
            @pl.when(chan + up < chan_count)
            def _():
                ahead(up, q).wait_recv()
    rest = pl.ds(1, groups - 1)
    pltpu.make_async_copy(send_v.at[rest], send_v.at[rest], send_sem).wait()
    for q in range(PARTS):
        for up in (1, 2):
            @pl.when(chan >= up)
            def _():
                ahead(up, q).wait_send()


def exchange(table, raw, mask, tm_count, chan_count, freq_count):
    groups = tm_count * freq_count
    width, length = raw.shape
    return pl.pallas_call(
        functools.partial(exchange_kernel, tm_count, chan_count, freq_count),
        out_shape=pltpu.VMEM((3, groups, 2 * ROWS, LANES), jnp.bfloat16),
        in_specs=[pl.BlockSpec(memory_space=pltpu.HBM)] * 3,
        out_specs=pl.BlockSpec(memory_space=pltpu.VMEM),
        scratch_shapes=[
            pltpu.VMEM(table.shape, jnp.bfloat16),
            pltpu.VMEM((width, length), jnp.bfloat16),
            pltpu.VMEM((1, width), jnp.int32),
            pltpu.VMEM((groups, 2 * ROWS, LANES), jnp.bfloat16),
            pltpu.SemaphoreType.DMA((2, TIME_CHUNKS)),
            pltpu.SemaphoreType.DMA,
            pltpu.SemaphoreType.DMA,
            pltpu.SemaphoreType.DMA((PARTS,)),
            pltpu.SemaphoreType.DMA((2, PARTS)),
            pltpu.SemaphoreType.DMA((2, PARTS)),
        ],
        compiler_params=pltpu.CompilerParams(
            collective_id=0, has_side_effects=True, vmem_limit_bytes=16 << 20
        ),
        name="exchange",
    )(*(pltpu.with_memory_space_constraint(x, pltpu.HBM) for x in (table, raw, mask)))


def channel_of(row):
    return row // 8 * 8 + 7 - row % 8


def band_kernel(blocks_ref, reach_ref, out_ref, right_v, left_v, reach_v, band_v, out_sem):
    depth = right_v.shape[0]
    row = lax.broadcasted_iota(jnp.int32, (LANES, LANES), 0)
    lane = lax.broadcasted_iota(jnp.int32, (LANES, LANES), 1)
    order = (channel_of(row) == lane).astype(jnp.bfloat16)
    for block in range(3):
        tiles = blocks_ref[block].astype(jnp.float32)
        for half in range(2):
            at = (2 * block + half) * LANES
            piece = tiles[:, half * ROWS:(half + 1) * ROWS, :]
            right_v[:, at:at + LANES] = piece.reshape(depth, LANES).astype(jnp.bfloat16)
            if block == 0:
                turned = jnp.concatenate([-piece[:, FB_DEV:], piece[:, :FB_DEV]], axis=1)
                for part, value in enumerate((piece, turned)):
                    left_v[part, at:at + LANES, :] = lax.dot_general(
                        order, value.reshape(depth, LANES).astype(jnp.bfloat16), (((1,), (1,)), ((), ())),
                        preferred_element_type=jnp.float32,
                    ).astype(jnp.bfloat16)
    reach_v[...] = jnp.broadcast_to(reach_ref[...], (LANES, 2 * LANES)).T

    column = lax.broadcasted_iota(jnp.int32, (LANES, depth), 1)
    backwards = 7 - lax.broadcasted_iota(jnp.int32, (8, LANES), 0)
    tiles = K // LANES
    copies = []
    for part in range(2):
        for which in range(FB_DEV):
            for half in range(2):
                rows = slice(half * LANES, (half + 1) * LANES)
                left = jnp.where(column % FB_DEV == which, left_v[part, rows, :], jnp.zeros((), jnp.bfloat16))
                product = jnp.concatenate([
                    jnp.dot(left, right_v[:, at:at + 2 * LANES], preferred_element_type=jnp.float32)
                    for at in range(0, 6 * LANES, 2 * LANES)
                ], axis=1)[:, half * LANES:half * LANES + K + LANES]
                for j in range(tiles):
                    here = product[:, j * LANES:(j + 1) * LANES]
                    beyond = product[:, (j + 1) * LANES:(j + 2) * LANES]
                    joined = jnp.where(lane >= channel_of(row), here, beyond)
                    band = jnp.concatenate([
                        jnp.take_along_axis(
                            pltpu.roll(joined[at:at + 8], (LANES - 7 - at) % LANES, 1, stride=1, stride_axis=0),
                            backwards, axis=0, mode="promise_in_bounds",
                        )
                        for at in range(0, LANES, 8)
                    ], axis=0)
                    band = jnp.where(lane + j * LANES <= reach_v[rows, :], band, 0.0)
                    band_v[part, which, rows, j * LANES:(j + 1) * LANES] = band.astype(jnp.bfloat16)
            copy = pltpu.make_async_copy(band_v.at[part, which], out_ref.at[part, which], out_sem.at[part, which])
            copy.start()
            copies.append(copy)
    for copy in copies:
        copy.wait()


def band_of(blocks, reach):
    depth = blocks.shape[1] * ROWS
    shape = (2, FB_DEV, 2 * LANES, K)
    return pl.pallas_call(
        band_kernel,
        out_shape=jax.ShapeDtypeStruct(shape, jnp.bfloat16),
        in_specs=[pl.BlockSpec(memory_space=pltpu.VMEM)] * 2,
        out_specs=pl.BlockSpec(memory_space=pl.ANY),
        scratch_shapes=[
            pltpu.VMEM((depth, 6 * LANES), jnp.bfloat16),
            pltpu.VMEM((2, 2 * LANES, depth), jnp.bfloat16),
            pltpu.VMEM((2 * LANES, LANES), jnp.int32),
            pltpu.VMEM(shape, jnp.bfloat16),
            pltpu.SemaphoreType.DMA((2, FB_DEV)),
        ],
        compiler_params=pltpu.CompilerParams(vmem_limit_bytes=32 << 20),
        name="band",
    )(blocks, reach)


def body(table, raw_record, good_mask, reach_limit):
    tm_count, chan_count, freq_count = (lax.axis_size(a) for a in ("tm", "chan", "freq"))
    width = raw_record.shape[1]
    blocks = exchange(table, raw_record[0], good_mask.reshape(1, width), tm_count, chan_count, freq_count)
    return band_of(blocks, reach_limit.reshape(1, width))


def solution(mesh):
    groups = mesh.shape["tm"] * mesh.shape["freq"]
    sharded = jax.shard_map(
        body,
        mesh=mesh,
        in_specs=(P(), P(("tm", "freq"), "chan", None), P("chan"), P("chan")),
        out_specs=P(None, ("tm", "freq"), "chan", None),
        check_vma=False,
    )

    def run(raw_record, good_mask, reach_limit):
        table = jnp.asarray(build_rows(groups, raw_record.shape[2]))
        return sharded(table, raw_record, good_mask, reach_limit)

    return run
```

time: 38.4 us -> 31.1 us (0.81)
  Pallas kernels: 38.3 us -> 31 us
    pallas_call x1, Pallas kernels: 6.36 us -> 2.17 us  [band_of(): pl.pallas_call(band_kernel, out_shape=jax.ShapeDtypeStruct(shape, jnp.bfl...]
    pallas_call x1, Pallas kernels: 31.9 us -> 28.8 us  [exchange(): pl.pallas_call(functools.partial(exchange_kernel, tm_count, chan_count, f...]
where the time goes in v2:
time: 31.1 us; the launch traced here: 31 us
  Pallas kernels  31 us (100%)
    pallas_call x1, Pallas kernels, exchange(): pl.pallas_call(functools.partial(exchange_kernel, tm_count, chan_count, f...  28.8 us
    pallas_call x1, Pallas kernels, band_of(): pl.pallas_call(band_kernel, out_shape=jax.ShapeDtypeStruct(shape, jnp.bfl...  2.17 us

profile of v2, /device:TPU:1, one launch (start us, length us, event | category | flops | bytes accessed | tf_op | source)
XLA Modules:
  0.0 31.0 jit_solution(5970825824173538933)
XLA Ops:
  0.0 0.0 copy-start
  0.0 28.8 %exchange.1.blocks_ref = bf16[3,32,16,128]{3,2,1,0:T(8,128)(2,1)S(1)} custom-call(bf16[32,256,128]{2,1,0:T(8,128)(2,1)} %constant.2.clone.table_ref, bf16[256,4096]{1,0:T(8,128)(2,1)} %bitcast.4, s32[1,256]{1,0:T(1,128)} %bitcast.5), custom_call_target="tpu_custom_call" | custom-call | tf_op jit(solution)/shard_map/exchange/pallas_call | solution.py:142
  28.8 0.0 copy-done
  28.9 2.2 %band.1 = bf16[2,4,256,512]{3,2,1,0:T(8,128)(2,1)} custom-call(bf16[3,32,16,128]{3,2,1,0:T(8,128)(2,1)S(1)} %exchange.1.blocks_ref, s32[1,256]{1,0:T(1,128)S(1)} %bitcast.3), custom_call_target="tpu_custom_call" | custom-call | tf_op jit(solution)/shard_map/band/pallas_call | solution.py:226
Async XLA Ops:
  0.0 28.8 %copy-start = (s32[256]{0:T(256)S(1)}, s32[256]{0:T(256)}, u32[]{:S(2)}) copy-start(s32[256]{0:T(256)} %param.6) | copy-start | bytes 3076

commit v3 on v2

--- a/solution.py
+++ b/solution.py
@@ -35,16 +35,21 @@
 
 
 def exchange_kernel(tm_count, chan_count, freq_count, table_ref, raw_ref, mask_ref, blocks_ref,
-                    table_v, raw_v, mask_v, send_v, load_sem, mask_sem, send_sem, recv_sem, ahead_send, ahead_recv):
+                    table_v, raw_v, mask_v, send_v, load_sem, mask_sem, send_sem, recv_sem, ahead_send, ahead_recv, relay_send, go_sem):
     tm, chan, freq = lax.axis_index("tm"), lax.axis_index("chan"), lax.axis_index("freq")
     groups = tm_count * freq_count
     per_part = groups // PARTS
 
-    peers = [(tm, lax.rem(freq + df, freq_count), 0, df) for df in range(1, freq_count)]
+    beside = [(tm, lax.rem(freq + df, freq_count), 0, df) for df in range(1, freq_count)]
+    peers = []
     for k in range(tm_count - 1):
         t = k + jnp.minimum(jnp.maximum(k + 1 - tm, 0), 1)
         rank = rank_of(lax.rem(tm - t + tm_count, tm_count), tm_count)
         peers += [(t, lax.rem(freq + df, freq_count), rank, df) for df in range(freq_count)]
+
+    low, high = 5 * tm_count // 16, 10 * tm_count // 16
+    split = (low + high) // 2
+    far = (tm >= low) & (tm < high)
 
     length = raw_ref.shape[1]
     step = length // TIME_CHUNKS
@@ -63,8 +68,30 @@
     mask_copy.start()
 
     barrier = pltpu.get_barrier_semaphore()
-    for t, f, _, _ in peers:
+
+    def greet(t, f):
         pl.semaphore_signal(barrier, inc=1, device_id=(t, chan, f), device_id_type=MESH)
+
+    @pl.when(tm < low)
+    def _():
+        for t, f, _, _ in beside + peers:
+            greet(t, f)
+
+    @pl.when(far)
+    def _():
+        for t in (*range(low), *range(high, tm_count)):
+            for f in range(freq_count):
+                greet(t, f)
+
+    @pl.when(tm >= high)
+    def _():
+        for t in (*range(low), *range(high, tm_count - 1)):
+            past = jnp.minimum(jnp.maximum(t + 1 - tm, 0), 1)
+            for f in range(freq_count):
+                greet(t + past, f)
+        for t, f, _, _ in beside:
+            greet(t, f)
+
     for up in (1, 2):
         @pl.when(chan + up < chan_count)
         def _():
@@ -91,17 +118,47 @@
     tiles = jnp.concatenate([white[:, :, :LANES], white[:, :, LANES:]], axis=1)
     send_v[...] = tiles.astype(jnp.bfloat16)
 
-    pl.semaphore_wait(barrier, groups - 1 + jnp.minimum(chan, 2))
-    for t, f, rank, df in peers:
-        pltpu.make_async_remote_copy(
-            src_ref=send_v.at[t * freq_count + f],
-            dst_ref=blocks_ref.at[0, rank * freq_count + df],
-            send_sem=send_sem,
-            recv_sem=recv_sem.at[rank * freq_count // per_part],
-            device_id=(t, chan, f),
-            device_id_type=MESH,
-        ).start()
+    def send(some):
+        for t, f, rank, df in some:
+            pltpu.make_async_remote_copy(
+                src_ref=send_v.at[t * freq_count + f],
+                dst_ref=blocks_ref.at[0, rank * freq_count + df],
+                send_sem=send_sem,
+                recv_sem=recv_sem.at[rank * freq_count // per_part],
+                device_id=(t, chan, f),
+                device_id_type=MESH,
+            ).start()
+
+    def let_go(planes):
+        for t in planes:
+            pl.semaphore_signal(go_sem, inc=1, device_id=(t, chan, freq), device_id_type=MESH)
+
+    @pl.when(far)
+    def _():
+        pl.semaphore_wait(barrier, low * freq_count + jnp.minimum(chan, 2))
+
+    @pl.when(jnp.logical_not(far))
+    def _():
+        pl.semaphore_wait(barrier, groups - 1 + jnp.minimum(chan, 2))
+
+    @pl.when(tm == low - 1)
+    def _():
+        let_go(range(low, split))
+
+    @pl.when(tm == high)
+    def _():
+        let_go(range(split, high))
+
+    send(peers[:low * freq_count])
+
+    @pl.when(far)
+    def _():
+        pl.semaphore_wait(go_sem, 1)
+
+    send(beside + peers[low * freq_count:])
     blocks_ref[0, 0] = send_v[tm * freq_count + freq]
+
+    odd = lax.rem(chan, 2) == 1
 
     def ahead(up, q):
         span = pl.ds(q * per_part, per_part)
@@ -118,22 +175,60 @@
         lo = 1 if q == 0 else q * per_part
         span = pl.ds(lo, (q + 1) * per_part - lo)
         pltpu.make_async_copy(blocks_ref.at[0, span], blocks_ref.at[0, span], recv_sem.at[q]).wait()
-        for up in (2, 1):
-            @pl.when(chan >= up)
-            def _():
-                ahead(up, q).start()
-    for q in range(PARTS):
-        for up in (1, 2):
-            @pl.when(chan + up < chan_count)
-            def _():
-                ahead(up, q).wait_recv()
+        @pl.when(odd & (chan >= 2))
+        def _():
+            ahead(2, q).start()
+
+        @pl.when(chan >= 1)
+        def _():
+            ahead(1, q).start()
+
+    passing = odd & (chan + 1 < chan_count)
+
+    def relay(q):
+        span = pl.ds(q * per_part, per_part)
+        return pltpu.make_async_remote_copy(
+            src_ref=blocks_ref.at[1, span],
+            dst_ref=blocks_ref.at[2, span],
+            send_sem=relay_send.at[q],
+            recv_sem=ahead_recv.at[1, q],
+            device_id=(tm, chan - 1, freq),
+            device_id_type=MESH,
+        )
+
+    @pl.when(passing)
+    def _():
+        for q in range(PARTS):
+            ahead(1, q).wait_recv()
+            relay(q).start()
+
+    @pl.when(jnp.logical_not(odd))
+    def _():
+        for q in range(PARTS):
+            ahead(1, q).wait_recv()
+
+    @pl.when(chan + 2 < chan_count)
+    def _():
+        for q in range(PARTS):
+            ahead(2, q).wait_recv()
+
     rest = pl.ds(1, groups - 1)
     pltpu.make_async_copy(send_v.at[rest], send_v.at[rest], send_sem).wait()
-    for q in range(PARTS):
-        for up in (1, 2):
-            @pl.when(chan >= up)
-            def _():
-                ahead(up, q).wait_send()
+
+    @pl.when(chan >= 1)
+    def _():
+        for q in range(PARTS):
+            ahead(1, q).wait_send()
+
+    @pl.when(odd & (chan >= 2))
+    def _():
+        for q in range(PARTS):
+            ahead(2, q).wait_send()
+
+    @pl.when(passing)
+    def _():
+        for q in range(PARTS):
+            relay(q).wait_send()
 
 
 def exchange(table, raw, mask, tm_count, chan_count, freq_count):
@@ -155,6 +250,8 @@
             pltpu.SemaphoreType.DMA((PARTS,)),
             pltpu.SemaphoreType.DMA((2, PARTS)),
             pltpu.SemaphoreType.DMA((2, PARTS)),
+            pltpu.SemaphoreType.DMA((PARTS,)),
+            pltpu.SemaphoreType.REGULAR,
         ],
         compiler_params=pltpu.CompilerParams(
             collective_id=0, has_side_effects=True, vmem_limit_bytes=16 << 20

time: 31.1 us -> 30.1 us (0.968)
  Pallas kernels: 31 us -> 30 us
    pallas_call x1, Pallas kernels: 28.8 us -> 27.8 us  [exchange(): pl.pallas_call(functools.partial(exchange_kernel, tm_count, chan_count, f...]
where the time goes in v3:
time: 30.1 us; the launch traced here: 30 us
  Pallas kernels  30 us (100%)
    pallas_call x1, Pallas kernels, exchange(): pl.pallas_call(functools.partial(exchange_kernel, tm_count, chan_count, f...  27.8 us
    pallas_call x1, Pallas kernels, band_of(): pl.pallas_call(band_kernel, out_shape=jax.ShapeDtypeStruct(shape, jnp.bfl...  2.16 us

profile of v3, /device:TPU:1, one launch (start us, length us, event | category | flops | bytes accessed | tf_op | source)
XLA Modules:
  0.0 30.0 jit_solution(12480143110775893945)
XLA Ops:
  0.0 0.0 copy-start
  0.0 27.8 %exchange.1.blocks_ref = bf16[3,32,16,128]{3,2,1,0:T(8,128)(2,1)S(1)} custom-call(bf16[32,256,128]{2,1,0:T(8,128)(2,1)} %constant.2.clone.table_ref, bf16[256,4096]{1,0:T(8,128)(2,1)} %bitcast.4, s32[1,256]{1,0:T(1,128)} %bitcast.5), custom_call_target="tpu_custom_call" | custom-call | tf_op jit(solution)/shard_map/exchange/pallas_call | solution.py:237
  27.9 0.0 copy-done
  27.9 2.2 %band.1 = bf16[2,4,256,512]{3,2,1,0:T(8,128)(2,1)} custom-call(bf16[3,32,16,128]{3,2,1,0:T(8,128)(2,1)S(1)} %exchange.1.blocks_ref, s32[1,256]{1,0:T(1,128)S(1)} %bitcast.3), custom_call_target="tpu_custom_call" | custom-call | tf_op jit(solution)/shard_map/band/pallas_call | solution.py:323
Async XLA Ops:
  0.0 27.9 %copy-start = (s32[256]{0:T(256)S(1)}, s32[256]{0:T(256)}, u32[]{:S(2)}) copy-start(s32[256]{0:T(256)} %param.6) | copy-start | bytes 3076

commit v4 on v3

--- a/solution.py
+++ b/solution.py
@@ -175,13 +175,13 @@
         lo = 1 if q == 0 else q * per_part
         span = pl.ds(lo, (q + 1) * per_part - lo)
         pltpu.make_async_copy(blocks_ref.at[0, span], blocks_ref.at[0, span], recv_sem.at[q]).wait()
-        @pl.when(odd & (chan >= 2))
-        def _():
-            ahead(2, q).start()
-
         @pl.when(chan >= 1)
         def _():
             ahead(1, q).start()
+
+        @pl.when((odd if q < PARTS - 1 else True) & (chan >= 2))
+        def _():
+            ahead(2, q).start()
 
     passing = odd & (chan + 1 < chan_count)
 
@@ -200,7 +200,8 @@
     def _():
         for q in range(PARTS):
             ahead(1, q).wait_recv()
-            relay(q).start()
+            if q < PARTS - 1:
+                relay(q).start()
 
     @pl.when(jnp.logical_not(odd))
     def _():
@@ -222,12 +223,16 @@
 
     @pl.when(odd & (chan >= 2))
     def _():
-        for q in range(PARTS):
+        for q in range(PARTS - 1):
             ahead(2, q).wait_send()
 
+    @pl.when(chan >= 2)
+    def _():
+        ahead(2, PARTS - 1).wait_send()
+
     @pl.when(passing)
     def _():
-        for q in range(PARTS):
+        for q in range(PARTS - 1):
             relay(q).wait_send()
 
 

time: 30.1 us -> 29.8 us (0.990)
    pallas_call x1, Pallas kernels: 27.8 us -> 27.5 us  [exchange(): pl.pallas_call(functools.partial(exchange_kernel, tm_count, chan_count, f...]
where the time goes in v4:
time: 29.8 us; the launch traced here: 29.7 us
  Pallas kernels  29.7 us (100%)
    pallas_call x1, Pallas kernels, exchange(): pl.pallas_call(functools.partial(exchange_kernel, tm_count, chan_count, f...  27.5 us
    pallas_call x1, Pallas kernels, band_of(): pl.pallas_call(band_kernel, out_shape=jax.ShapeDtypeStruct(shape, jnp.bfl...  2.17 us

profile of v4, /device:TPU:1, one launch (start us, length us, event | category | flops | bytes accessed | tf_op | source)
XLA Modules:
  0.0 29.7 jit_solution(10162258409975599040)
XLA Ops:
  0.0 0.0 copy-start
  0.0 27.5 %exchange.1.blocks_ref = bf16[3,32,16,128]{3,2,1,0:T(8,128)(2,1)S(1)} custom-call(bf16[32,256,128]{2,1,0:T(8,128)(2,1)} %constant.2.clone.table_ref, bf16[256,4096]{1,0:T(8,128)(2,1)} %bitcast.4, s32[1,256]{1,0:T(1,128)} %bitcast.5), custom_call_target="tpu_custom_call" | custom-call | tf_op jit(solution)/shard_map/exchange/pallas_call | solution.py:242
  27.5 0.0 copy-done
  27.5 2.2 %band.1 = bf16[2,4,256,512]{3,2,1,0:T(8,128)(2,1)} custom-call(bf16[3,32,16,128]{3,2,1,0:T(8,128)(2,1)S(1)} %exchange.1.blocks_ref, s32[1,256]{1,0:T(1,128)S(1)} %bitcast.3), custom_call_target="tpu_custom_call" | custom-call | tf_op jit(solution)/shard_map/band/pallas_call | solution.py:328
Async XLA Ops:
  0.0 27.5 %copy-start = (s32[256]{0:T(256)S(1)}, s32[256]{0:T(256)}, u32[]{:S(2)}) copy-start(s32[256]{0:T(256)} %param.6) | copy-start | bytes 3076

commit v5 on v4

--- a/solution.py
+++ b/solution.py
@@ -34,8 +34,12 @@
     return jnp.maximum(jnp.minimum(2 * distance - 1, 2 * (count - distance)), 0)
 
 
-def exchange_kernel(tm_count, chan_count, freq_count, table_ref, raw_ref, mask_ref, blocks_ref,
-                    table_v, raw_v, mask_v, send_v, load_sem, mask_sem, send_sem, recv_sem, ahead_send, ahead_recv, relay_send, go_sem):
+def channel_of(row):
+    return row // 8 * 8 + 7 - row % 8
+
+
+def exchange_kernel(tm_count, chan_count, freq_count, table_ref, raw_ref, mask_ref, right_ref, left_ref,
+                    table_v, raw_v, mask_v, send_v, blocks_ref, load_sem, mask_sem, send_sem, recv_sem, ahead_send, ahead_recv, relay_send, go_sem):
     tm, chan, freq = lax.axis_index("tm"), lax.axis_index("chan"), lax.axis_index("freq")
     groups = tm_count * freq_count
     per_part = groups // PARTS
@@ -179,7 +183,7 @@
         def _():
             ahead(1, q).start()
 
-        @pl.when((odd if q < PARTS - 1 else True) & (chan >= 2))
+        @pl.when((odd if q < 2 else True) & (chan >= 2))
         def _():
             ahead(2, q).start()
 
@@ -196,11 +200,32 @@
             device_id_type=MESH,
         )
 
+    depth = groups * ROWS
+
+    def lay_out(block):
+        tiles = blocks_ref[block].astype(jnp.float32)
+        for half in range(2):
+            at = (2 * block + half) * LANES
+            piece = tiles[:, half * ROWS:(half + 1) * ROWS, :]
+            right_ref[:, at:at + LANES] = piece.reshape(depth, LANES).astype(jnp.bfloat16)
+            if block == 0:
+                row = lax.broadcasted_iota(jnp.int32, (LANES, LANES), 0)
+                lane = lax.broadcasted_iota(jnp.int32, (LANES, LANES), 1)
+                order = (channel_of(row) == lane).astype(jnp.bfloat16)
+                turned = jnp.concatenate([-piece[:, FB_DEV:], piece[:, :FB_DEV]], axis=1)
+                for part, value in enumerate((piece, turned)):
+                    left_ref[part, at:at + LANES, :] = lax.dot_general(
+                        order, value.reshape(depth, LANES).astype(jnp.bfloat16), (((1,), (1,)), ((), ())),
+                        preferred_element_type=jnp.float32,
+                    ).astype(jnp.bfloat16)
+
+    lay_out(0)
+
     @pl.when(passing)
     def _():
         for q in range(PARTS):
             ahead(1, q).wait_recv()
-            if q < PARTS - 1:
+            if q < 2:
                 relay(q).start()
 
     @pl.when(jnp.logical_not(odd))
@@ -208,11 +233,15 @@
         for q in range(PARTS):
             ahead(1, q).wait_recv()
 
+    lay_out(1)
+
     @pl.when(chan + 2 < chan_count)
     def _():
         for q in range(PARTS):
             ahead(2, q).wait_recv()
 
+    lay_out(2)
+
     rest = pl.ds(1, groups - 1)
     pltpu.make_async_copy(send_v.at[rest], send_v.at[rest], send_sem).wait()
 
@@ -223,16 +252,17 @@
 
     @pl.when(odd & (chan >= 2))
     def _():
-        for q in range(PARTS - 1):
+        for q in range(2):
             ahead(2, q).wait_send()
 
     @pl.when(chan >= 2)
     def _():
-        ahead(2, PARTS - 1).wait_send()
+        for q in range(2, PARTS):
+            ahead(2, q).wait_send()
 
     @pl.when(passing)
     def _():
-        for q in range(PARTS - 1):
+        for q in range(2):
             relay(q).wait_send()
 
 
@@ -241,14 +271,18 @@
     width, length = raw.shape
     return pl.pallas_call(
         functools.partial(exchange_kernel, tm_count, chan_count, freq_count),
-        out_shape=pltpu.VMEM((3, groups, 2 * ROWS, LANES), jnp.bfloat16),
+        out_shape=(
+            pltpu.VMEM((groups * ROWS, 6 * LANES), jnp.bfloat16),
+            pltpu.VMEM((2, 2 * LANES, groups * ROWS), jnp.bfloat16),
+        ),
         in_specs=[pl.BlockSpec(memory_space=pltpu.HBM)] * 3,
-        out_specs=pl.BlockSpec(memory_space=pltpu.VMEM),
+        out_specs=(pl.BlockSpec(memory_space=pltpu.VMEM),) * 2,
         scratch_shapes=[
             pltpu.VMEM(table.shape, jnp.bfloat16),
             pltpu.VMEM((width, length), jnp.bfloat16),
             pltpu.VMEM((1, width), jnp.int32),
             pltpu.VMEM((groups, 2 * ROWS, LANES), jnp.bfloat16),
+            pltpu.VMEM((3, groups, 2 * ROWS, LANES), jnp.bfloat16),
             pltpu.SemaphoreType.DMA((2, TIME_CHUNKS)),
             pltpu.SemaphoreType.DMA,
             pltpu.SemaphoreType.DMA,
@@ -265,43 +299,26 @@
     )(*(pltpu.with_memory_space_constraint(x, pltpu.HBM) for x in (table, raw, mask)))
 
 
-def channel_of(row):
-    return row // 8 * 8 + 7 - row % 8
-
-
-def band_kernel(blocks_ref, reach_ref, out_ref, right_v, left_v, reach_v, band_v, out_sem):
-    depth = right_v.shape[0]
+def band_kernel(right_ref, left_ref, reach_ref, out_ref, reach_v, band_v, out_sem):
+    depth = right_ref.shape[0]
     row = lax.broadcasted_iota(jnp.int32, (LANES, LANES), 0)
     lane = lax.broadcasted_iota(jnp.int32, (LANES, LANES), 1)
-    order = (channel_of(row) == lane).astype(jnp.bfloat16)
-    for block in range(3):
-        tiles = blocks_ref[block].astype(jnp.float32)
-        for half in range(2):
-            at = (2 * block + half) * LANES
-            piece = tiles[:, half * ROWS:(half + 1) * ROWS, :]
-            right_v[:, at:at + LANES] = piece.reshape(depth, LANES).astype(jnp.bfloat16)
-            if block == 0:
-                turned = jnp.concatenate([-piece[:, FB_DEV:], piece[:, :FB_DEV]], axis=1)
-                for part, value in enumerate((piece, turned)):
-                    left_v[part, at:at + LANES, :] = lax.dot_general(
-                        order, value.reshape(depth, LANES).astype(jnp.bfloat16), (((1,), (1,)), ((), ())),
-                        preferred_element_type=jnp.float32,
-                    ).astype(jnp.bfloat16)
     reach_v[...] = jnp.broadcast_to(reach_ref[...], (LANES, 2 * LANES)).T
 
-    column = lax.broadcasted_iota(jnp.int32, (LANES, depth), 1)
+    column = lax.broadcasted_iota(jnp.int32, (2 * LANES, depth), 1)
     backwards = 7 - lax.broadcasted_iota(jnp.int32, (8, LANES), 0)
     tiles = K // LANES
     copies = []
     for part in range(2):
         for which in range(FB_DEV):
+            left = jnp.where(column % FB_DEV == which, left_ref[part], jnp.zeros((), jnp.bfloat16))
+            whole = jnp.concatenate([
+                jnp.dot(left, right_ref[:, at:at + 2 * LANES], preferred_element_type=jnp.float32)
+                for at in range(0, 6 * LANES, 2 * LANES)
+            ], axis=1)
             for half in range(2):
                 rows = slice(half * LANES, (half + 1) * LANES)
-                left = jnp.where(column % FB_DEV == which, left_v[part, rows, :], jnp.zeros((), jnp.bfloat16))
-                product = jnp.concatenate([
-                    jnp.dot(left, right_v[:, at:at + 2 * LANES], preferred_element_type=jnp.float32)
-                    for at in range(0, 6 * LANES, 2 * LANES)
-                ], axis=1)[:, half * LANES:half * LANES + K + LANES]
+                product = whole[rows, half * LANES:half * LANES + K + LANES]
                 for j in range(tiles):
                     here = product[:, j * LANES:(j + 1) * LANES]
                     beyond = product[:, (j + 1) * LANES:(j + 2) * LANES]
@@ -322,31 +339,28 @@
         copy.wait()
 
 
-def band_of(blocks, reach):
-    depth = blocks.shape[1] * ROWS
+def band_of(right, left, reach):
     shape = (2, FB_DEV, 2 * LANES, K)
     return pl.pallas_call(
         band_kernel,
         out_shape=jax.ShapeDtypeStruct(shape, jnp.bfloat16),
-        in_specs=[pl.BlockSpec(memory_space=pltpu.VMEM)] * 2,
+        in_specs=[pl.BlockSpec(memory_space=pltpu.VMEM)] * 3,
         out_specs=pl.BlockSpec(memory_space=pl.ANY),
         scratch_shapes=[
-            pltpu.VMEM((depth, 6 * LANES), jnp.bfloat16),
-            pltpu.VMEM((2, 2 * LANES, depth), jnp.bfloat16),
             pltpu.VMEM((2 * LANES, LANES), jnp.int32),
             pltpu.VMEM(shape, jnp.bfloat16),
             pltpu.SemaphoreType.DMA((2, FB_DEV)),
         ],
         compiler_params=pltpu.CompilerParams(vmem_limit_bytes=32 << 20),
         name="band",
-    )(blocks, reach)
+    )(right, left, reach)
 
 
 def body(table, raw_record, good_mask, reach_limit):
     tm_count, chan_count, freq_count = (lax.axis_size(a) for a in ("tm", "chan", "freq"))
     width = raw_record.shape[1]
-    blocks = exchange(table, raw_record[0], good_mask.reshape(1, width), tm_count, chan_count, freq_count)
-    return band_of(blocks, reach_limit.reshape(1, width))
+    right, left = exchange(table, raw_record[0], good_mask.reshape(1, width), tm_count, chan_count, freq_count)
+    return band_of(right, left, reach_limit.reshape(1, width))
 
 
 def solution(mesh):

time: 29.8 us -> 29.6 us (level)
  Pallas kernels: 29.7 us -> 29.4 us
where the time goes in v5:
time: 29.6 us; the launch traced here: 29.4 us
  Pallas kernels  29.4 us (99%)
    pallas_call x1, Pallas kernels, exchange(): pl.pallas_call(functools.partial(exchange_kernel, tm_count, chan_count, f...  27.4 us
    pallas_call x1, Pallas kernels, band_of(): pl.pallas_call(band_kernel, out_shape=jax.ShapeDtypeStruct(shape, jnp.bfl...  2.04 us

profile of v5, /device:TPU:1, one launch (start us, length us, event | category | flops | bytes accessed | tf_op | source)
XLA Modules:
  0.0 29.4 jit_solution(7249451906098678986)
XLA Ops:
  0.0 0.0 copy-start
  0.0 27.4 %exchange.1 = (bf16[256,768]{1,0:T(8,128)(2,1)S(1)}, bf16[2,256,256]{2,1,0:T(8,128)(2,1)S(1)}) custom-call(bf16[32,256,128]{2,1,0:T(8,128)(2,1)} %constant.2.clone.table_ref, bf16[256,4096]{1,0:T(8,128)(2,1)} %bitcast.4, s32[1,256]{1,0:T(1,128)} %bitcast.5), custom_call_target="tpu_custom_call" | custom-call | tf_op jit(solution)/shard_map/exchange/pallas_call | solution.py:272
  27.4 0.0 copy-done
  27.4 2.0 %band.1 = bf16[2,4,256,512]{3,2,1,0:T(8,128)(2,1)} custom-call(bf16[256,768]{1,0:T(8,128)(2,1)S(1)} %get-tuple-element.7.right_ref, bf16[2,256,256]{2,1,0:T(8,128)(2,1)S(1)} %get-tuple-element.8.left_ref, s32[1,256]{1,0:T(1,128)S(1)} %bitcast.3), custom_call_target="tpu_custom_call" | custom-call | tf_op jit(solution)/shard_map/band/pallas_call | solution.py:344
Async XLA Ops:
  0.0 27.4 %copy-start = (s32[256]{0:T(256)S(1)}, s32[256]{0:T(256)}, u32[]{:S(2)}) copy-start(s32[256]{0:T(256)} %param.6) | copy-start | bytes 3076

commit v6 on v5

--- a/solution.py
+++ b/solution.py
@@ -13,7 +13,7 @@
 FB_DEV = 4
 ROWS = 2 * FB_DEV
 LANES = 128
-TIME_CHUNKS = 4
+TIME_CHUNKS = 2
 PARTS = 4
 MESH = pl.DeviceIdType.MESH
 
@@ -65,12 +65,6 @@
             pltpu.make_async_copy(table_ref.at[runs], table_v.at[runs], load_sem.at[0, i]),
             pltpu.make_async_copy(raw_ref.at[:, span], raw_v.at[:, span], load_sem.at[1, i]),
         ))
-    for pair in loads:
-        for copy in pair:
-            copy.start()
-    mask_copy = pltpu.make_async_copy(mask_ref, mask_v, mask_sem)
-    mask_copy.start()
-
     barrier = pltpu.get_barrier_semaphore()
 
     def greet(t, f):
@@ -80,12 +74,6 @@
     def _():
         for t, f, _, _ in beside + peers:
             greet(t, f)
-
-    @pl.when(far)
-    def _():
-        for t in (*range(low), *range(high, tm_count)):
-            for f in range(freq_count):
-                greet(t, f)
 
     @pl.when(tm >= high)
     def _():
@@ -100,6 +88,18 @@
         @pl.when(chan + up < chan_count)
         def _():
             pl.semaphore_signal(barrier, inc=1, device_id=(tm, chan + up, freq), device_id_type=MESH)
+
+    for pair in loads:
+        for copy in pair:
+            copy.start()
+    mask_copy = pltpu.make_async_copy(mask_ref, mask_v, mask_sem)
+    mask_copy.start()
+
+    @pl.when(far)
+    def _():
+        for t in (*range(low), *range(high, tm_count)):
+            for f in range(freq_count):
+                greet(t, f)
 
     for up in (1, 2):
         @pl.when(chan + up >= chan_count)
@@ -219,14 +219,18 @@
                         preferred_element_type=jnp.float32,
                     ).astype(jnp.bfloat16)
 
+    @pl.when(passing)
+    def _():
+        for q in range(2):
+            ahead(1, q).wait_recv()
+            relay(q).start()
+
     lay_out(0)
 
     @pl.when(passing)
     def _():
-        for q in range(PARTS):
+        for q in range(2, PARTS):
             ahead(1, q).wait_recv()
-            if q < 2:
-                relay(q).start()
 
     @pl.when(jnp.logical_not(odd))
     def _():

time: 29.6 us -> 29.7 us (level)
  no operation moved by 1% of the time
where the time goes in v6:
time: 29.7 us; the launch traced here: 29.6 us
  Pallas kernels  29.6 us (100%)
    pallas_call x1, Pallas kernels, exchange(): pl.pallas_call(functools.partial(exchange_kernel, tm_count, chan_count, f...  27.5 us
    pallas_call x1, Pallas kernels, band_of(): pl.pallas_call(band_kernel, out_shape=jax.ShapeDtypeStruct(shape, jnp.bfl...  2.04 us

profile of v6, /device:TPU:1, one launch (start us, length us, event | category | flops | bytes accessed | tf_op | source)
XLA Modules:
  0.0 29.6 jit_solution(13464854463884626366)
XLA Ops:
  0.0 0.0 copy-start
  0.0 27.5 %exchange.1 = (bf16[256,768]{1,0:T(8,128)(2,1)S(1)}, bf16[2,256,256]{2,1,0:T(8,128)(2,1)S(1)}) custom-call(bf16[32,256,128]{2,1,0:T(8,128)(2,1)} %constant.2.clone.table_ref, bf16[256,4096]{1,0:T(8,128)(2,1)} %bitcast.4, s32[1,256]{1,0:T(1,128)} %bitcast.5), custom_call_target="tpu_custom_call" | custom-call | tf_op jit(solution)/shard_map/exchange/pallas_call | solution.py:276
  27.5 0.0 copy-done
  27.5 2.0 %band.1 = bf16[2,4,256,512]{3,2,1,0:T(8,128)(2,1)} custom-call(bf16[256,768]{1,0:T(8,128)(2,1)S(1)} %get-tuple-element.7.right_ref, bf16[2,256,256]{2,1,0:T(8,128)(2,1)S(1)} %get-tuple-element.8.left_ref, s32[1,256]{1,0:T(1,128)S(1)} %bitcast.3), custom_call_target="tpu_custom_call" | custom-call | tf_op jit(solution)/shard_map/band/pallas_call | solution.py:348
Async XLA Ops:
  0.0 27.5 %copy-start = (s32[256]{0:T(256)S(1)}, s32[256]{0:T(256)}, u32[]{:S(2)}) copy-start(s32[256]{0:T(256)} %param.6) | copy-start | bytes 3076
